TPU v7x, 32 devices: a whole 2x2x4 slice. The times are simulated.
32 devices in a mesh: ctx: 8 (over z, y), hg: 4 (over x, core).
Axes of the slice: x: 2, y: 2, z: 4, core: 2. Of those that a mesh axis runs over, the one named last changes fastest.
Arguments:
- query: bfloat16 [1024, 5120], P('ctx', 'hg'), may hold values from -6 to 6
- key: bfloat16 [1024, 5120], P('ctx', 'hg'), may hold values from -6 to 6
- value: bfloat16 [1024, 5120], P('ctx', 'hg'), may hold values from -6 to 6
- gate_logit: float32 [1024, 40], P('ctx', 'hg'), may hold values from -40 to 10
- exponent: int32 [40], P('hg'), may hold values from 0 to 6
- norm_gain: float32 [5120], P('hg'), may hold values from 0.5 to 1.5
- kv_weight: bfloat16 [5120, 2048], P('hg'), may hold values from -0.078125 to 0.078125
- cross_query: bfloat16 [1024, 5120], P('ctx', 'hg'), may hold values from -256 to 256
Outputs:
- retained: bfloat16 [1024, 5120], P('ctx', 'hg')
- attended: bfloat16 [1024, 5120], P('ctx', 'hg')
All inputs are finite; a program needn't handle non-finite values.
Results may differ from a plain program's by a relative error of at most 0.013.
The roundings to bfloat16 on the way count: a program that leaves them out, or rounds other values in their place, can miss the bound.
Values may be sent and summed in bfloat16 or wider, within the bound.
A program may use at most 128 MiB of HBM per device.

v0:
```python
import math

import jax
import jax.numpy as jnp
from jax import lax
from jax.sharding import PartitionSpec as P

HD = 128


def carried_in(value, axis, join, neutral):
    count, mine = (lax.axis_size(axis), lax.axis_index(axis))
    pieces = jax.tree.map(lambda part: lax.all_gather(part, axis), value)
    so_far = jax.tree.map(
        lambda part, zero: jnp.full_like(part, 0) + jnp.asarray(zero, part.dtype), value, neutral
    )

    def lap(position, so_far):
        longer = join(so_far, jax.tree.map(lambda part: part[position], pieces))
        return jax.tree.map(lambda new, old: jnp.where(position < mine, new, old), longer, so_far)

    return lax.fori_loop(0, count - 1, lap, so_far)


def combine(earlier, later):
    return (earlier[0] * later[0], later[0][:, None, None] * earlier[1] + later[1])


def body(query, key, value, gate_logit, exponent, norm_gain, kv_weight, cross_query):
    tok, width = query.shape
    head_size = HD
    heads = width // head_size
    scale = head_size ** (-0.5)
    rank = lax.axis_index("ctx")
    rate = jnp.exp2(-exponent.astype(jnp.float32))
    log_gate = jax.nn.log_sigmoid(gate_logit) * rate[None, :]
    cumul = jnp.cumsum(log_gate, axis=0)
    total = cumul[-1]
    q_heads = query.reshape(tok, heads, head_size)
    k_heads = key.reshape(tok, heads, head_size)
    v_heads = value.reshape(tok, heads, head_size)
    v_float = v_heads.astype(jnp.float32)
    scaled_keys = (
        k_heads.astype(jnp.float32) * (jnp.exp(total[None, :] - cumul) * scale)[:, :, None]
    )
    fresh = jnp.einsum("thd,the->hde", scaled_keys, v_float, precision=lax.Precision.HIGHEST)
    identity = (
        jnp.ones((heads,), jnp.float32),
        jnp.zeros((heads, head_size, head_size), jnp.float32),
    )
    entering = carried_in((jnp.exp(total), fresh), "ctx", combine, identity)[1]
    lower = jnp.arange(tok)[:, None] >= jnp.arange(tok)[None, :]
    diff = jnp.transpose(cumul[:, None, :] - cumul[None, :, :], (2, 0, 1))
    decay = jnp.where(lower[None], jnp.exp(jnp.where(lower[None], diff, 0.0)), 0.0)
    scores = jnp.einsum("thd,shd->hts", q_heads, k_heads, preferred_element_type=jnp.float32)
    weight = (scores * decay * scale).astype(jnp.bfloat16)
    local = jnp.einsum("hts,shd->thd", weight, v_heads, preferred_element_type=jnp.float32)
    carried = (
        jnp.einsum(
            "thd,hde->the", q_heads.astype(jnp.float32), entering, precision=lax.Precision.HIGHEST
        )
        * jnp.exp(cumul)[:, :, None]
    )
    out = local + carried
    mean = jnp.mean(out, axis=-1, keepdims=True)
    var = jnp.mean((out - mean) ** 2, axis=-1, keepdims=True)
    normed = (out - mean) / jnp.sqrt(var + 1e-06) * norm_gain.reshape(heads, head_size)
    retained = normed.astype(jnp.bfloat16).reshape(tok, width)
    partial_value = jnp.dot(retained, kv_weight, preferred_element_type=jnp.float32)
    share = partial_value.shape[1] // lax.axis_size("hg")
    summed = lax.psum(partial_value, "hg")
    owned = lax.dynamic_slice_in_dim(summed, lax.axis_index("hg") * share, share, 1)
    cache = owned.astype(jnp.bfloat16)
    kv_heads = share // (2 * head_size)
    group = heads // kv_heads
    cross = cross_query.reshape(tok, kv_heads, group, head_size)
    q_pos = rank * tok + jnp.arange(tok)
    start_state = (
        jnp.full((kv_heads, group, tok), -1e30, jnp.float32),
        jnp.zeros((kv_heads, group, tok), jnp.float32),
        jnp.zeros((tok, kv_heads, group, head_size), jnp.float32),
    )
    piece = lax.all_gather(cache, "ctx", axis=0, tiled=True)
    rows = piece.shape[0]
    block = math.gcd(rows, 512)
    tiles = piece.reshape(rows // block, block, kv_heads, 2, head_size)

    def inner(state, item):
        top, denom, accum = state
        index, tile = item
        keys_t = tile[:, :, 0, :]
        vals_t = tile[:, :, 1, :]
        score = (
            jnp.einsum("tkgd,skd->kgts", cross, keys_t, preferred_element_type=jnp.float32) * scale
        )
        k_pos = index * block + jnp.arange(block)
        mask = k_pos[None, :] <= q_pos[:, None]
        score = jnp.where(mask, score, -1e30)
        new_top = jnp.maximum(top, jnp.max(score, axis=-1))
        expo = jnp.where(mask, jnp.exp(score - new_top[..., None]), 0.0)
        factor = jnp.exp(top - new_top)
        denom = denom * factor + jnp.sum(expo, axis=-1)
        contrib = jnp.einsum(
            "kgts,skd->tkgd", expo.astype(jnp.bfloat16), vals_t, preferred_element_type=jnp.float32
        )
        accum = accum * jnp.transpose(factor, (2, 0, 1))[..., None] + contrib
        return ((new_top, denom, accum), None)

    steps = jnp.arange(rows // block, dtype=jnp.int32)
    result, unused = lax.scan(inner, start_state, (steps, tiles))
    top, denom, accum = result
    attended = accum / jnp.transpose(denom, (2, 0, 1))[..., None]
    return (retained, attended.reshape(tok, width).astype(jnp.bfloat16))


def solution(mesh):
    in_specs = (
        P("ctx", "hg"),
        P("ctx", "hg"),
        P("ctx", "hg"),
        P("ctx", "hg"),
        P("hg"),
        P("hg"),
        P("hg", None),
        P("ctx", "hg"),
    )
    out_specs = (P("ctx", "hg"), P("ctx", "hg"))
    return jax.shard_map(body, mesh=mesh, in_specs=in_specs, out_specs=out_specs, check_vma=False)
```

profile of v0, /device:TPU:0, one launch (start us, length us, event | category | flops | bytes accessed | tf_op | source)
XLA Modules:
  0.0 208.1 jit_solution(7080567937442938854)
XLA Ops:
  7.2 0.0 copy-start
  7.2 0.0 all-gather.7.cloned.1.call-start
  7.2 0.7 multiply_exponential_fusion
  7.9 0.8 fusion.39
  8.7 0.1 copy.49
  8.8 0.2 reduce_window_sum.11
  9.0 0.1 copy.53
  9.1 1.2 copy.46
  10.3 1.2 copy.52
  11.5 1.7 fusion.25
  13.2 0.0 all-gather.7.cloned.1.call-update
  13.2 0.0 all-gather.5.cloned.1.call-start
  13.2 0.1 copy.57
  13.3 0.0 copy-done
  13.3 0.2 copy.45
  13.5 0.1 copy.50
  13.6 22.4 %all-gather.1 = f32[8,1,10]{2,1,0:T(1,128)S(1)} all-gather(f32[1,1,10]{2,1,0:T(1,128)S(1)} %get-tuple-element.253), channel_id=1, replica_groups=mesh['ctx'=8,'hg'=4] {'ctx'}, dimensions={0}, use_global_device_ids=true | all-gather | bytes 360 | tf_op jit(solution)/shard_map/all_gather | solution.py:13
  36.0 66.3 %all-gather.7.cloned.1.call-done = f32[80,128,128]{2,1,0:T(8,128)} async-done(((f32[10,128,128]{2,1,0:T(8,128)}), f32[80,128,128]{2,1,0:T(8,128)}) %all-gather.7.cloned.1.call-update) | async-done | bytes 5242896 | tf_op jit(solution)/shard_map/all_gather | solution.py:13
  102.3 8.9 %while.29 = (s32[]{:T(128)}, f32[10,128,128]{2,1,0:T(8,128)S(1)}, s32[]{:T(128)}, f32[8,10]{1,0:T(8,128)S(1)}, f32[8,10,128,128]{3,2,1,0:T(8,128)}, /*index=5*/s32[]{:T(128)}, s32[]{:T(128)}) while((s32[]{:T(128)}, f32[10,128,128]{2,1,0:T(8,128)S(1)}, s32[]{:T(128)}, f32[8,10]{1,0:T(8,128)S(1)}, f32[8,10,128,128]{3,2,1,0:T(8,128)}, ...), condition=%wide.region_2.3_spmd.clone, body=%wide.region_1.2_spmd.clone.sunk | while | flops 655364 | bytes 1966305 | solution.py:22
  102.3 1.2 fusion.62
  103.6 1.2 fusion.62
  104.9 1.2 fusion.62
  106.1 1.2 fusion.62
  107.4 1.2 fusion.62
  108.7 1.2 fusion.62
  109.9 1.2 fusion.62
  111.2 0.0 copy-start.4
  111.2 0.7 fusion.21
  111.9 0.6 fusion.43
  112.5 0.1 multiply_reduce_fusion
  112.6 0.2 multiply_convert_fusion
  112.8 0.0 copy-start.1
  112.9 3.4 %fusion.44 = f32[128,2048]{1,0:T(8,128)S(1)} fusion(bf16[128,1280]{0,1:T(8,128)(2,1)S(1)} %bitcast.104, bf16[1280,2048]{1,0:T(8,128)(2,1)} %param.18), kind=kOutput, calls=%fused_computation.68 | convolution fusion | flops 671088640 | bytes 6619136 | tf_op jit(solution)/shard_map/dot_general | solution.py:69
  116.3 25.2 %all-reduce.1 = bf16[128,2048]{1,0:T(8,128)(2,1)S(1)} all-reduce(f32[128,2048]{1,0:T(8,128)S(1)} %fusion.44), channel_id=1, replica_groups=mesh['ctx'=8,'hg'=4] {'hg'}, use_global_device_ids=true, to_apply=%region_5.6 | all-reduce | flops 262144 | bytes 1572864 | tf_op jit(solution)/shard_map/psum | solution.py:71
  141.5 0.7 dynamic-slice_convert_fusion
  142.2 0.0 all-gather.5.cloned.1.call-update
  142.2 0.0 copy-done.1
  142.2 0.2 copy.58
  142.4 0.2 copy.60
  142.7 0.9 copy.61
  143.6 37.8 %all-gather.5.cloned.1.call-done = bf16[1024,512]{1,0:T(8,128)(2,1)} async-done(((bf16[128,512]{1,0:T(8,128)(2,1)}), bf16[1024,512]{1,0:T(8,128)(2,1)}) %all-gather.5.cloned.1.call-update) | async-done | bytes 1048592 | tf_op jit(solution)/shard_map/all_gather | solution.py:83
  181.4 2.2 %reshape.88 = bf16[2,512,2,2,128]{4,3,2,1,0:T(2,128)(2,1)} reshape(bf16[1024,512]{1,0:T(8,128)(2,1)} %all-gather.5.cloned.1.call-done) | data formatting | bytes 2097152 | tf_op jit(solution)/shard_map/reshape | solution.py:86
  183.5 0.5 iota.26
  184.0 15.1 %while.30 = (s32[]{:T(128)}, f32[2,5,128]{2,1,0:T(8,128)S(1)}, f32[2,5,128]{2,1,0:T(8,128)}, f32[128,2,5,128]{0,3,2,1:T(8,128)}, s32[2]{0:T(128)}, /*index=5*/bf...) while((s32[]{:T(128)}, f32[2,5,128]{2,1,0:T(8,128)S(1)}, ...), condition=%wide.region_9.10_spmd.clone, body=%wide.region_6.9_spmd.clone.sunk | while | flops 344629376 | bytes 12520661 | solution.py:110
  184.0 1.2 dynamic_slice.41
  185.9 0.1 broadcast_compare_fusion.2
  186.0 1.4 constant_dynamic-slice_fusion.2
  187.4 0.1 copy.77
  187.5 0.5 fusion.65
  188.1 1.7 fusion.69
  189.8 0.6 fusion.67
  190.4 0.1 copy-done.2
  190.5 0.6 copy-done.3
  191.1 1.2 dynamic_slice.41
  192.9 0.1 broadcast_compare_fusion.2
  193.0 1.4 constant_dynamic-slice_fusion.2
  194.5 0.1 copy.77
  194.5 0.5 fusion.65
  195.1 2.8 %fusion.69 = f32[128,2,5,128]{0,3,2,1:T(8,128)} fusion(f32[2,512,128,5]{2,1,3,0:T(8,128)S(1)} %get-tuple-element.342, f32[2,5,128]{2,1,0:T(8,128)S(1)} %get-tuple-element.388, pred[128,512]{0,1:T(8,128)(4,1)S(1)} %broadcast_compare_fusion.2, f32[128,2,5,128]{0,3,2,1:T(8,128)} %get-tuple-element.379, f32[128,2,5]{0,2,1:T(8,128)S(1)} %get-tuple-element.343, ...), kind=kOutput, calls=%fused_computation.12.clone.1 | convolution fusion | flops 171540480 | bytes 4276225 | tf_op jit(solution)/shard_map/while/body/eval_jaxpr/kgts,skd->tkgd/dot_general | solution.py:103
  197.9 0.6 fusion.67
  198.5 0.1 copy-done.2
  198.6 0.6 copy-done.3
  199.2 1.2 divide_convert_fusion
  200.3 0.9 copy.62
  (31 shorter events, 0.2 us)
Async XLA Ops:
  7.2 6.1 %copy-start = (bf16[128,1280]{1,0:T(8,128)(2,1)S(1)}, bf16[128,1280]{1,0:T(8,128)(2,1)}, u32[]{:S(2)}) copy-start(bf16[128,1280]{1,0:T(8,128)(2,1)} %param.12) | copy-start | bytes 983044
  7.2 95.1 %all-gather.7.cloned.1.call-start = ((), (), s32[]{:S(2)}) async-start(), calls=%async_computation.1 | async-start | bytes 5898240 | tf_op jit(solution)/shard_map/all_gather | solution.py:13
  13.2 168.2 %all-gather.5.cloned.1.call-start = ((), (), s32[]{:S(2)}) async-start(), calls=%async_computation | async-start | bytes 1179648 | tf_op jit(solution)/shard_map/all_gather | solution.py:83
  111.2 1.4 copy-start.4
  112.8 29.4 %copy-start.1 = (bf16[128,1280]{1,0:T(8,128)(2,1)S(1)}, bf16[128,1280]{1,0:T(8,128)(2,1)}, u32[]{:S(2)}) copy-start(bf16[128,1280]{1,0:T(8,128)(2,1)} %param.19) | copy-start | bytes 983044
  189.8 0.7 copy-start.2
  190.5 0.6 copy-start.3
  197.9 0.7 copy-start.2
  198.6 0.6 copy-start.3
Sparse Core Ops, SparseCore 0:
  13.3 88.9 all-gather.6
  142.3 39.0 all-gather.4
where the time goes:
time: 209 us; the launch traced here: 208 us
  waiting for transfers between devices  104 us (50%)
  blocking collectives  47.6 us (23%)
  local copies, waits for them, and re-layouts  15.3 us (7%)
  between operations  14.2 us (7%)
  other arithmetic  13.4 us (6%)
  matrix products  11.9 us (6%)
    all_gather x1, waiting for transfers between devices, carried_in(): pieces = jax.tree.map(lambda part: lax.all_gather(part, axis), value)  66.3 us
    all_gather x1, waiting for transfers between devices, body(): piece = lax.all_gather(cache, 'ctx', axis=0, tiled=True)  37.8 us
    psum x1, blocking collectives, body(): summed = lax.psum(partial_value, 'hg')  25.2 us
    all_gather x1, blocking collectives, carried_in(): pieces = jax.tree.map(lambda part: lax.all_gather(part, axis), value)  22.4 us
    select_n x7, other arithmetic, lap(): jnp.where(position < mine, new, old)  8.62 us
    dynamic_slice x6, local copies, waits for them, and re-layouts, body(): result, unused = lax.scan(inner, start_state, (steps, tiles))  5.43 us
    unnamed x13, local copies, waits for them, and re-layouts  4.89 us
    dot_general x2, matrix products, inner(): jnp.einsum('kgts,skd->tkgd', expo.astype(jnp.bfloat16), vals_t, preferred...  4.48 us
  transfers between devices with their start and end apart: 2, of which 2 were waited for; matrix products, arithmetic and copies ran while one was open for 1% of the time, Pallas kernels for 0%

commit v1 on v0

v1 whole, which is shorter than its diff:
```python
import functools

import jax
import jax.numpy as jnp
from jax import lax
from jax.experimental import pallas as pl
from jax.experimental.pallas import tpu as pltpu
from jax.sharding import PartitionSpec as P

HD = 128
F32 = jnp.float32
BF16 = jnp.bfloat16
MESH = pl.DeviceIdType.MESH


def dot(a, b, dims=((1,), (0,))):
    return lax.dot_general(a, b, (dims, ((), ())), preferred_element_type=F32)


def split(x):
    hi = x.astype(BF16)
    return hi, (x - hi.astype(F32)).astype(BF16)


def kernel(
    nz, nhg,
    q_ref, k_ref, v_ref, gate_ref, expo_ref, gain_ref, w_hbm, cq_ref,
    ret_ref, att_ref,
    w_vm, bcol, brow, dtot_ref, local_ref,
    own_f, send_f, recv_f, send_s, recv_s, send_e, recv_e,
    p1_send, p1_recv, p2_send, p2_recv, own_p,
    kv, cross, top_ref, den_ref, acc_ref,
    w_sem, fs, fr, ss, sr, es, er, p1s, p1r, p2s, p2r, zs, zr, ys, yr,
):
    tok, width = q_ref.shape
    heads = width // HD
    half = heads // 2
    share = w_vm.shape[1] // nhg
    kvh = share // (2 * HD)
    group = heads // kvh
    rows = group * tok
    scale = HD ** (-0.5)
    me = lax.axis_index("ctx")
    g = lax.axis_index("hg")
    z = me // 2
    y = me % 2
    partner = {"ctx": me + 1 - 2 * y, "hg": g}
    ahead = {"ctx": me + 2, "hg": g}
    behind = {"ctx": me - 2, "hg": g}
    g1 = g + 1 - 2 * (g % 2)
    g2 = (g + nhg // 2) % nhg
    g3 = (g1 + nhg // 2) % nhg
    near = {"ctx": me, "hg": g1}
    far = {"ctx": me, "hg": g2}
    first = z == 0
    last = z == nz - 1

    w_copy = pltpu.make_async_copy(w_hbm, w_vm, w_sem)
    w_copy.start()

    barrier = pltpu.get_barrier_semaphore()
    for who in (partner, near, far):
        pl.semaphore_signal(barrier, inc=1, device_id=who, device_id_type=MESH)

    @pl.when(jnp.logical_not(first))
    def _():
        pl.semaphore_signal(barrier, inc=1, device_id=behind, device_id_type=MESH)

    @pl.when(jnp.logical_not(last))
    def _():
        pl.semaphore_signal(barrier, inc=1, device_id=ahead, device_id_type=MESH)

    def send(src, dst, s_sem, r_sem, who):
        return pltpu.make_async_remote_copy(
            src_ref=src, dst_ref=dst, send_sem=s_sem, recv_sem=r_sem,
            device_id=who, device_id_type=MESH,
        )

    def cols(h, n=HD):
        return pl.ds(pl.multiple_of(h * n, n), n)

    x = gate_ref[...]
    rate = jnp.exp2(-expo_ref[...].astype(F32))
    log_gate = (jnp.minimum(x, 0.0) - jnp.log1p(jnp.exp(-jnp.abs(x)))) * rate
    log_gate = jnp.concatenate([log_gate, jnp.zeros((tok, HD - heads), F32)], axis=1)
    r_id = lax.broadcasted_iota(jnp.int32, (tok, tok), 0)
    c_id = lax.broadcasted_iota(jnp.int32, (tok, tok), 1)
    lower = r_id >= c_id
    cumul = lax.dot_general(
        lower.astype(F32), log_gate, (((1,), (0,)), ((), ())),
        precision=lax.Precision.HIGHEST, preferred_element_type=F32,
    )
    brow[...] = jnp.transpose(cumul)
    for h in range(heads):
        bcol[h] = jnp.broadcast_to(cumul[:, h : h + 1], (tok, HD))
        dtot_ref[h] = jnp.broadcast_to(jnp.exp(cumul[tok - 1 : tok, h : h + 1]), (8, HD))

    def fresh(h, out, j):
        total = bcol[h, tok - 1 : tok, :]
        keys = k_ref[:, cols(h)].astype(F32) * (jnp.exp(total - bcol[h]) * scale)
        hi, lo = split(keys)
        vals = v_ref[:, cols(h)]
        dims = ((0,), (0,))
        out[j, :HD, :] = dot(hi, vals, dims) + dot(lo, vals, dims)
        out[j, HD:, :] = dtot_ref[h]

    pl.semaphore_wait(barrier, 3 + jnp.where(first, 0, 1) + jnp.where(last, 0, 1))

    for j in range(half):
        fresh((1 - y) * half + j, send_f, j)
        send(send_f.at[j], recv_f.at[j], fs.at[j], fr.at[j], partner).start()
    for j in range(half):
        fresh(y * half + j, own_f, j)

    def pair(j):
        mine, his = own_f[j, :HD, :], recv_f[j, :HD, :]
        dm, dh = own_f[j, HD : HD + 1, :], recv_f[j, HD : HD + 1, :]
        even = y == 0
        f0, f1 = jnp.where(even, mine, his), jnp.where(even, his, mine)
        d0, d1 = jnp.where(even, dm, dh), jnp.where(even, dh, dm)
        return f0, f1, d0, d1

    def f_copy(j):
        return send(send_f.at[j], recv_f.at[j], fs.at[j], fr.at[j], partner)

    def s_copy(j):
        return send(send_s.at[j], recv_s.at[j], ss.at[j], sr.at[j], ahead)

    def e_copy(j):
        return send(send_e.at[j], recv_e.at[j], es.at[j], er.at[j], partner)

    @pl.when(first)
    def _():
        recv_s[...] = jnp.zeros_like(recv_s)

    for j in range(half):
        f_copy(j).wait_recv()
        f0, f1, d0, d1 = pair(j)
        send_s[j] = d1 * f0 + f1

        @pl.when(first)
        def _():
            s_copy(j).start()

    for h in range(heads):
        diff = jnp.minimum(bcol[h] - brow[h : h + 1, :], 0.0)
        decay = jnp.where(lower, jnp.exp(diff), 0.0)
        at = slice(h * HD, (h + 1) * HD)
        score = dot(q_ref[:, at], k_ref[:, at], ((1,), (1,)))
        weight = (score * decay * scale).astype(BF16)
        local_ref[h] = dot(weight, v_ref[:, at])

    for h in range(heads):
        c, i = h // group, h % group
        cross[c, i * tok : (i + 1) * tok, :] = cq_ref[:, h * HD : (h + 1) * HD]
    top_ref[...] = jnp.full_like(top_ref, -1e30)
    den_ref[...] = jnp.zeros_like(den_ref)
    acc_ref[...] = jnp.zeros_like(acc_ref)

    def finish(h, state):
        hi, lo = split(state)
        qh = q_ref[:, cols(h)]
        out = local_ref[h] + (dot(qh, hi) + dot(qh, lo)) * jnp.exp(bcol[h])
        mean = jnp.mean(out, axis=-1, keepdims=True)
        out = out - mean
        var = jnp.mean(out * out, axis=-1, keepdims=True)
        out = out / jnp.sqrt(var + 1e-06) * gain_ref[:, cols(h)]
        ret_ref[:, cols(h)] = out.astype(BF16)

    for j in range(half):
        @pl.when(jnp.logical_not(first))
        def _():
            s_copy(j).wait_recv()
            _, _, d0, d1 = pair(j)
            send_s[j] = (d0 * d1) * recv_s[j] + send_s[j]

            @pl.when(jnp.logical_not(last))
            def _():
                s_copy(j).start()

        f0, _, d0, _ = pair(j)
        s = recv_s[j]
        e1 = d0 * s + f0
        send_e[j] = jnp.where(y == 0, e1, s)
        e_copy(j).start()
        finish(y * half + j, jnp.where(y == 0, s, e1))
    for j in range(half):
        e_copy(j).wait_recv()
        finish((1 - y) * half + j, recv_e[j])

    w_copy.wait()
    wide = 2 * HD

    def p1_copy(c, b):
        return send(p1_send.at[c, b], p1_recv.at[c, b], p1s.at[c, b], p1r.at[c, b], near)

    def p2_copy(c):
        return send(p2_send.at[c], p2_recv.at[c], p2s.at[c], p2r.at[c], far)

    def part(dest, c):
        return dot(ret_ref[...], w_vm[:, cols(dest * kvh + c, wide)])

    for c in range(kvh):
        for b, dest in ((0, g3), (1, g1)):
            p1_send[c, b] = part(dest, c)
            p1_copy(c, b).start()
    for c in range(kvh):
        p2_send[c] = part(g2, c)
    for c in range(kvh):
        p1_copy(c, 0).wait_recv()
        p2_send[c] = p2_send[c] + p1_recv[c, 0]
        p2_copy(c).start()
    for c in range(kvh):
        own_p[c] = part(g, c)
        p1_copy(c, 1).wait_recv()
        own_p[c] = own_p[c] + p1_recv[c, 1]

    def spot(block, c):
        return kv.at[c, pl.ds(pl.multiple_of(block * tok, tok), tok), :]

    def z_copy(zz, c):
        at = spot(2 * zz + y, c)
        return send(at, at, zs.at[zz, c], zr.at[zz, c], ahead)

    def y_copy(zz, c):
        at = spot(2 * zz + y, c)
        return send(at, at, ys.at[zz, c], yr.at[zz, c], partner)

    def y_arrived(zz, c):
        at = spot(2 * zz + 1 - y, c)
        return send(at, at, ys.at[zz, c], yr.at[zz, c], partner)

    def attend(zz, c, masked):
        both = kv[c, pl.ds(pl.multiple_of(zz * 2 * tok, 2 * tok), 2 * tok), :]
        keys, vals = both[:, :HD], both[:, HD:]
        for i in range(group):
            at = slice(i * tok, (i + 1) * tok)
            score = dot(cross[c, at, :], keys, ((1,), (1,))) * scale
            if masked:
                q_pos = y * tok + lax.broadcasted_iota(jnp.int32, (tok, 2 * tok), 0)
                keep = lax.broadcasted_iota(jnp.int32, (tok, 2 * tok), 1) <= q_pos
                score = jnp.where(keep, score, -1e30)
            old = top_ref[c, at, :]
            new = jnp.maximum(old, jnp.max(score, axis=-1, keepdims=True))
            factor = jnp.exp(old - new)
            top_ref[c, at, :] = new
            new2 = jnp.concatenate([new, new], axis=1)
            expo = jnp.exp(score - new2)
            if masked:
                expo = jnp.where(keep, expo, 0.0)
            den_ref[c, at, :] = den_ref[c, at, :] * factor + (expo[:, :HD] + expo[:, HD:])
            acc_ref[c, at, :] = acc_ref[c, at, :] * factor + dot(expo.astype(BF16), vals)

    def earlier(zz, carry):
        for c in range(kvh):
            z_copy(zz, c).wait_recv()

            @pl.when(jnp.logical_not(last))
            def _():
                z_copy(zz, c).start()

            y_copy(zz, c).start()
        for c in range(kvh):
            y_arrived(zz, c).wait_recv()
            attend(zz, c, False)
        return carry

    lax.fori_loop(0, z, earlier, 0)

    for c in range(kvh):
        p2_copy(c).wait_recv()
        spot(me, c)[...] = (own_p[c] + p2_recv[c]).astype(BF16)

        @pl.when(y == 0)
        def _():
            y_copy(z, c).start()
            spot(me + 1, c)[...] = jnp.zeros((tok, wide), BF16)

        @pl.when(jnp.logical_not(last))
        def _():
            z_copy(z, c).start()

    for c in range(kvh):
        @pl.when(y == 1)
        def _():
            y_arrived(z, c).wait_recv()

        attend(z, c, True)
    for h in range(heads):
        c, i = h // group, h % group
        at = slice(i * tok, (i + 1) * tok)
        total = jnp.sum(den_ref[c, at, :], axis=-1, keepdims=True)
        att_ref[:, h * HD : (h + 1) * HD] = (acc_ref[c, at, :] / total).astype(BF16)

    for j in range(half):
        f_copy(j).wait_send()
        e_copy(j).wait_send()

        @pl.when(jnp.logical_not(last))
        def _():
            s_copy(j).wait_send()

    for c in range(kvh):
        p1_copy(c, 0).wait_send()
        p1_copy(c, 1).wait_send()
        p2_copy(c).wait_send()

        @pl.when(y == 0)
        def _():
            y_copy(z, c).wait_send()

        @pl.when(jnp.logical_not(last))
        def _():
            z_copy(z, c).wait_send()

    def drain(zz, carry):
        for c in range(kvh):
            y_copy(zz, c).wait_send()

            @pl.when(jnp.logical_not(last))
            def _():
                z_copy(zz, c).wait_send()

        return carry

    lax.fori_loop(0, z, drain, 0)


def body(nctx, nhg, query, key, value, gate_logit, exponent, norm_gain, kv_weight, cross_query):
    tok, width = query.shape
    heads = width // HD
    half = heads // 2
    nz = nctx // 2
    share = kv_weight.shape[1] // nhg
    kvh = share // (2 * HD)
    rows = heads // kvh * tok
    vmem = pl.BlockSpec(memory_space=pltpu.VMEM)
    dma = pltpu.SemaphoreType.DMA
    return pl.pallas_call(
        functools.partial(kernel, nz, nhg),
        out_shape=(
            jax.ShapeDtypeStruct((tok, width), BF16),
            jax.ShapeDtypeStruct((tok, width), BF16),
        ),
        in_specs=[vmem] * 6 + [pl.BlockSpec(memory_space=pl.ANY), vmem],
        out_specs=(vmem, vmem),
        scratch_shapes=[
            pltpu.VMEM(kv_weight.shape, BF16),
            pltpu.VMEM((heads, tok, HD), F32),
            pltpu.VMEM((HD, tok), F32),
            pltpu.VMEM((heads, 8, HD), F32),
            pltpu.VMEM((heads, tok, HD), F32),
            pltpu.VMEM((half, HD + 8, HD), F32),
            pltpu.VMEM((half, HD + 8, HD), F32),
            pltpu.VMEM((half, HD + 8, HD), F32),
            pltpu.VMEM((half, HD, HD), F32),
            pltpu.VMEM((half, HD, HD), F32),
            pltpu.VMEM((half, HD, HD), F32),
            pltpu.VMEM((half, HD, HD), F32),
            pltpu.VMEM((kvh, 2, tok, 2 * HD), F32),
            pltpu.VMEM((kvh, 2, tok, 2 * HD), F32),
            pltpu.VMEM((kvh, tok, 2 * HD), F32),
            pltpu.VMEM((kvh, tok, 2 * HD), F32),
            pltpu.VMEM((kvh, tok, 2 * HD), F32),
            pltpu.VMEM((kvh, nctx * tok, 2 * HD), BF16),
            pltpu.VMEM((kvh, rows, HD), BF16),
            pltpu.VMEM((kvh, rows, HD), F32),
            pltpu.VMEM((kvh, rows, HD), F32),
            pltpu.VMEM((kvh, rows, HD), F32),
            dma,
            dma((half,)), dma((half,)), dma((half,)), dma((half,)), dma((half,)), dma((half,)),
            dma((kvh, 2)), dma((kvh, 2)), dma((kvh,)), dma((kvh,)),
            dma((nz, kvh)), dma((nz, kvh)), dma((nz, kvh)), dma((nz, kvh)),
        ],
        compiler_params=pltpu.CompilerParams(
            collective_id=0, has_side_effects=True, vmem_limit_bytes=48 * 1024 * 1024
        ),
    )(
        query, key, value, gate_logit, exponent.reshape(1, heads),
        norm_gain.reshape(1, width), kv_weight, cross_query,
    )


def solution(mesh):
    spec = P("ctx", "hg")
    in_specs = (spec, spec, spec, spec, P("hg"), P("hg"), P("hg", None), spec)
    return jax.shard_map(
        functools.partial(body, mesh.shape["ctx"], mesh.shape["hg"]),
        mesh=mesh, in_specs=in_specs, out_specs=(spec, spec), check_vma=False,
    )
```

time: 209 us -> 66.7 us (0.32)
  the two profiles are of different devices: /device:TPU:0 before, /device:TPU:28 now
where the time goes in v1:
time: 66.7 us; the launch traced here: 66.4 us
  Pallas kernels  58.2 us (87%)
  local copies, waits for them, and re-layouts  7.49 us (11%)
    pallas_call x1, Pallas kernels, body(): pl.pallas_call(functools.partial(kernel, nz, nhg), out_shape=(jax.ShapeDt...  58.2 us
    unnamed x13, local copies, waits for them, and re-layouts  6.79 us

profile of v1, /device:TPU:28, one launch (start us, length us, event | category | flops | bytes accessed | tf_op | source)
XLA Modules:
  0.0 66.4 jit_solution(1448300503611623067)
XLA Ops:
  0.6 0.7 %reshape.11.gain_ref = f32[1,1280]{1,0:T(1,128)S(1)} reshape(f32[1280]{0:T(1024)} %param.13) | data formatting | bytes 10240 | tf_op jit(solution)/shard_map/reshape | solution.py:380
  1.3 0.8 %copy.10.gate_ref = f32[128,10]{1,0:T(8,128)S(1)} copy(f32[128,10]{0,1:T(8,128)} %param.11) | data formatting | bytes 10240 | tf_op args[3]
  2.1 0.0 copy-start
  2.1 1.0 %copy-done = bf16[128,1280]{1,0:T(8,128)(2,1)S(1)} copy-done((bf16[128,1280]{1,0:T(8,128)(2,1)S(1)}, bf16[128,1280]{1,0:T(8,128)(2,1)}, u32[]{:S(2)}) %copy-start) | copy-done | bytes 327704
  3.1 0.0 copy-start.1
  3.1 1.0 %copy-done.1 = bf16[128,1280]{1,0:T(8,128)(2,1)S(1)} copy-done((bf16[128,1280]{1,0:T(8,128)(2,1)S(1)}, bf16[128,1280]{1,0:T(8,128)(2,1)}, u32[]{:S(2)}) %copy-start.1) | copy-done | bytes 327704
  4.1 0.0 copy-start.2
  4.1 1.0 %copy-done.2 = bf16[128,1280]{1,0:T(8,128)(2,1)S(1)} copy-done((bf16[128,1280]{1,0:T(8,128)(2,1)S(1)}, bf16[128,1280]{1,0:T(8,128)(2,1)}, u32[]{:S(2)}) %copy-start.2) | copy-done | bytes 327704
  5.1 0.0 copy-start.3
  5.1 1.0 %copy-done.3 = bf16[128,1280]{1,0:T(8,128)(2,1)S(1)} copy-done((bf16[128,1280]{1,0:T(8,128)(2,1)S(1)}, bf16[128,1280]{1,0:T(8,128)(2,1)}, u32[]{:S(2)}) %copy-start.3) | copy-done | bytes 327704
  6.0 0.0 copy-start.4
  6.0 0.7 copy-done.4
  6.7 58.2 %shard_map.95 = (bf16[128,1280]{1,0:T(8,128)(2,1)S(1)}, bf16[128,1280]{1,0:T(8,128)(2,1)S(1)}) custom-call(bf16[128,1280]{1,0:T(8,128)(2,1)S(1)} %copy-done, bf16[128,1280]{1,0:T(8,128)(2,1)S(1)} %copy-done.1, bf16[128,1280]{1,0:T(8,128)(2,1)S(1)} %copy-done.2, f32[128,10]{1,0:T(8,128)S(1)} %copy.10.gate_ref, s32[1,10]{1,0:T(1,128)S(1)} %bitcast.1, ...), custom_call_target="tpu_custom_call" | custom-call | tf_op jit(solution)/shard_map/pallas_call | solution.py:339
  64.9 0.7 %copy.13 = bf16[128,1280]{1,0:T(8,128)(2,1)} copy(bf16[128,1280]{1,0:T(8,128)(2,1)S(1)} %get-tuple-element.4) | data formatting | bytes 655360
  65.6 0.7 %copy.14 = bf16[128,1280]{1,0:T(8,128)(2,1)} copy(bf16[128,1280]{1,0:T(8,128)(2,1)S(1)} %get-tuple-element.5) | data formatting | bytes 655360
Async XLA Ops:
  2.1 1.0 %copy-start = (bf16[128,1280]{1,0:T(8,128)(2,1)S(1)}, bf16[128,1280]{1,0:T(8,128)(2,1)}, u32[]{:S(2)}) copy-start(bf16[128,1280]{1,0:T(8,128)(2,1)} %q_ref.1) | copy-start | bytes 983044
  3.1 1.0 %copy-start.1 = (bf16[128,1280]{1,0:T(8,128)(2,1)S(1)}, bf16[128,1280]{1,0:T(8,128)(2,1)}, u32[]{:S(2)}) copy-start(bf16[128,1280]{1,0:T(8,128)(2,1)} %k_ref.1) | copy-start | bytes 983044
  4.1 1.0 %copy-start.2 = (bf16[128,1280]{1,0:T(8,128)(2,1)S(1)}, bf16[128,1280]{1,0:T(8,128)(2,1)}, u32[]{:S(2)}) copy-start(bf16[128,1280]{1,0:T(8,128)(2,1)} %v_ref.1) | copy-start | bytes 983044
  5.1 1.0 %copy-start.3 = (bf16[128,1280]{1,0:T(8,128)(2,1)S(1)}, bf16[128,1280]{1,0:T(8,128)(2,1)}, u32[]{:S(2)}) copy-start(bf16[128,1280]{1,0:T(8,128)(2,1)} %cq_ref.1) | copy-start | bytes 983044
  6.0 0.7 copy-start.4

commit v2 on v1

--- a/solution.py
+++ b/solution.py
@@ -24,13 +24,14 @@
 
 def kernel(
     nz, nhg,
-    q_ref, k_ref, v_ref, gate_ref, expo_ref, gain_ref, w_hbm, cq_ref,
+    q_hbm, k_hbm, v_hbm, gate_hbm, expo_hbm, gain_hbm, w_hbm, cq_hbm,
     ret_ref, att_ref,
+    q_ref, k_ref, v_ref, cq_ref, gate_ref, expo_ref, gain_ref, gate_pad,
     w_vm, bcol, brow, dtot_ref, local_ref,
     own_f, send_f, recv_f, send_s, recv_s, send_e, recv_e,
     p1_send, p1_recv, p2_send, p2_recv, own_p,
     kv, cross, top_ref, den_ref, acc_ref,
-    w_sem, fs, fr, ss, sr, es, er, p1s, p1r, p2s, p2r, zs, zr, ys, yr,
+    in_sem, fs, fr, ss, sr, es, er, p1s, p1r, p2s, p2r, zs, zr, ys, yr,
 ):
     tok, width = q_ref.shape
     heads = width // HD
@@ -55,8 +56,16 @@
     first = z == 0
     last = z == nz - 1
 
-    w_copy = pltpu.make_async_copy(w_hbm, w_vm, w_sem)
-    w_copy.start()
+    copies = [
+        pltpu.make_async_copy(src, dst, in_sem.at[i])
+        for i, (src, dst) in enumerate((
+            (gate_hbm, gate_ref), (expo_hbm, expo_ref), (k_hbm, k_ref), (v_hbm, v_ref),
+            (q_hbm, q_ref), (cq_hbm, cq_ref), (gain_hbm, gain_ref), (w_hbm, w_vm),
+        ))
+    ]
+    for copy in copies:
+        copy.start()
+    gate_copy, expo_copy, k_copy, v_copy, q_copy, cq_copy, gain_copy, w_copy = copies
 
     barrier = pltpu.get_barrier_semaphore()
     for who in (partner, near, far):
@@ -79,10 +88,14 @@
     def cols(h, n=HD):
         return pl.ds(pl.multiple_of(h * n, n), n)
 
+    gate_copy.wait()
+    expo_copy.wait()
     x = gate_ref[...]
     rate = jnp.exp2(-expo_ref[...].astype(F32))
-    log_gate = (jnp.minimum(x, 0.0) - jnp.log1p(jnp.exp(-jnp.abs(x)))) * rate
-    log_gate = jnp.concatenate([log_gate, jnp.zeros((tok, HD - heads), F32)], axis=1)
+    rate = jnp.concatenate([rate, jnp.zeros((1, HD - heads), F32)], axis=1)
+    gate_pad[...] = jnp.zeros_like(gate_pad)
+    gate_pad[:heads, :] = jnp.minimum(x, 0.0) - jnp.log1p(jnp.exp(-jnp.abs(x)))
+    log_gate = jnp.transpose(gate_pad[...]) * rate
     r_id = lax.broadcasted_iota(jnp.int32, (tok, tok), 0)
     c_id = lax.broadcasted_iota(jnp.int32, (tok, tok), 1)
     lower = r_id >= c_id
@@ -106,6 +119,8 @@
 
     pl.semaphore_wait(barrier, 3 + jnp.where(first, 0, 1) + jnp.where(last, 0, 1))
 
+    k_copy.wait()
+    v_copy.wait()
     for j in range(half):
         fresh((1 - y) * half + j, send_f, j)
         send(send_f.at[j], recv_f.at[j], fs.at[j], fr.at[j], partner).start()
@@ -142,6 +157,7 @@
         def _():
             s_copy(j).start()
 
+    q_copy.wait()
     for h in range(heads):
         diff = jnp.minimum(bcol[h] - brow[h : h + 1, :], 0.0)
         decay = jnp.where(lower, jnp.exp(diff), 0.0)
@@ -150,6 +166,8 @@
         weight = (score * decay * scale).astype(BF16)
         local_ref[h] = dot(weight, v_ref[:, at])
 
+    cq_copy.wait()
+    gain_copy.wait()
     for h in range(heads):
         c, i = h // group, h % group
         cross[c, i * tok : (i + 1) * tok, :] = cq_ref[:, h * HD : (h + 1) * HD]
@@ -164,9 +182,10 @@
         mean = jnp.mean(out, axis=-1, keepdims=True)
         out = out - mean
         var = jnp.mean(out * out, axis=-1, keepdims=True)
-        out = out / jnp.sqrt(var + 1e-06) * gain_ref[:, cols(h)]
+        out = out / jnp.sqrt(var + 1e-06) * gain_ref[pl.ds(h, 1), :]
         ret_ref[:, cols(h)] = out.astype(BF16)
 
+    lag = min(2, half)
     for j in range(half):
         @pl.when(jnp.logical_not(first))
         def _():
@@ -184,8 +203,12 @@
         send_e[j] = jnp.where(y == 0, e1, s)
         e_copy(j).start()
         finish(y * half + j, jnp.where(y == 0, s, e1))
-    for j in range(half):
+        if j >= lag:
+            e_copy(j - lag).wait_recv()
+            finish((1 - y) * half + j - lag, recv_e[j - lag])
+    for j in range(half - lag, half):
         e_copy(j).wait_recv()
+    for j in range(half - lag, half):
         finish((1 - y) * half + j, recv_e[j])
 
     w_copy.wait()
@@ -233,23 +256,21 @@
     def attend(zz, c, masked):
         both = kv[c, pl.ds(pl.multiple_of(zz * 2 * tok, 2 * tok), 2 * tok), :]
         keys, vals = both[:, :HD], both[:, HD:]
-        for i in range(group):
-            at = slice(i * tok, (i + 1) * tok)
-            score = dot(cross[c, at, :], keys, ((1,), (1,))) * scale
-            if masked:
-                q_pos = y * tok + lax.broadcasted_iota(jnp.int32, (tok, 2 * tok), 0)
-                keep = lax.broadcasted_iota(jnp.int32, (tok, 2 * tok), 1) <= q_pos
-                score = jnp.where(keep, score, -1e30)
-            old = top_ref[c, at, :]
-            new = jnp.maximum(old, jnp.max(score, axis=-1, keepdims=True))
-            factor = jnp.exp(old - new)
-            top_ref[c, at, :] = new
-            new2 = jnp.concatenate([new, new], axis=1)
-            expo = jnp.exp(score - new2)
-            if masked:
-                expo = jnp.where(keep, expo, 0.0)
-            den_ref[c, at, :] = den_ref[c, at, :] * factor + (expo[:, :HD] + expo[:, HD:])
-            acc_ref[c, at, :] = acc_ref[c, at, :] * factor + dot(expo.astype(BF16), vals)
+        score = dot(cross[c], keys, ((1,), (1,))) * scale
+        if masked:
+            q_pos = y * tok + lax.broadcasted_iota(jnp.int32, (tok, 2 * tok), 0)
+            keep = lax.broadcasted_iota(jnp.int32, (tok, 2 * tok), 1) <= q_pos
+            keep = jnp.concatenate([jnp.where(keep, 1.0, 0.0)] * group, axis=0) > 0.5
+            score = jnp.where(keep, score, -1e30)
+        old = top_ref[c]
+        new = jnp.maximum(old, jnp.max(score, axis=-1, keepdims=True))
+        factor = jnp.exp(old - new)
+        top_ref[c] = new
+        expo = jnp.exp(score - jnp.concatenate([new, new], axis=1))
+        if masked:
+            expo = jnp.where(keep, expo, 0.0)
+        den_ref[c] = den_ref[c] * factor + (expo[:, :HD] + expo[:, HD:])
+        acc_ref[c] = acc_ref[c] * factor + dot(expo.astype(BF16), vals)
 
     def earlier(zz, carry):
         for c in range(kvh):
@@ -265,7 +286,7 @@
             attend(zz, c, False)
         return carry
 
-    lax.fori_loop(0, z, earlier, 0)
+    lax.fori_loop(0, z - 1, earlier, 0)
 
     for c in range(kvh):
         p2_copy(c).wait_recv()
@@ -279,6 +300,10 @@
         @pl.when(jnp.logical_not(last))
         def _():
             z_copy(z, c).start()
+
+    @pl.when(jnp.logical_not(first))
+    def _():
+        earlier(z - 1, 0)
 
     for c in range(kvh):
         @pl.when(y == 1)
@@ -335,6 +360,7 @@
     kvh = share // (2 * HD)
     rows = heads // kvh * tok
     vmem = pl.BlockSpec(memory_space=pltpu.VMEM)
+    hbm = pl.BlockSpec(memory_space=pltpu.HBM)
     dma = pltpu.SemaphoreType.DMA
     return pl.pallas_call(
         functools.partial(kernel, nz, nhg),
@@ -342,9 +368,17 @@
             jax.ShapeDtypeStruct((tok, width), BF16),
             jax.ShapeDtypeStruct((tok, width), BF16),
         ),
-        in_specs=[vmem] * 6 + [pl.BlockSpec(memory_space=pl.ANY), vmem],
+        in_specs=[hbm] * 8,
         out_specs=(vmem, vmem),
         scratch_shapes=[
+            pltpu.VMEM((tok, width), BF16),
+            pltpu.VMEM((tok, width), BF16),
+            pltpu.VMEM((tok, width), BF16),
+            pltpu.VMEM((tok, width), BF16),
+            pltpu.VMEM((heads, tok), F32),
+            pltpu.VMEM((1, heads), jnp.int32),
+            pltpu.VMEM((heads, HD), F32),
+            pltpu.VMEM((HD, tok), F32),
             pltpu.VMEM(kv_weight.shape, BF16),
             pltpu.VMEM((heads, tok, HD), F32),
             pltpu.VMEM((HD, tok), F32),
@@ -367,17 +401,17 @@
             pltpu.VMEM((kvh, rows, HD), F32),
             pltpu.VMEM((kvh, rows, HD), F32),
             pltpu.VMEM((kvh, rows, HD), F32),
-            dma,
+            dma((8,)),
             dma((half,)), dma((half,)), dma((half,)), dma((half,)), dma((half,)), dma((half,)),
             dma((kvh, 2)), dma((kvh, 2)), dma((kvh,)), dma((kvh,)),
             dma((nz, kvh)), dma((nz, kvh)), dma((nz, kvh)), dma((nz, kvh)),
         ],
         compiler_params=pltpu.CompilerParams(
-            collective_id=0, has_side_effects=True, vmem_limit_bytes=48 * 1024 * 1024
+            collective_id=0, has_side_effects=True, vmem_limit_bytes=56 * 1024 * 1024
         ),
     )(
-        query, key, value, gate_logit, exponent.reshape(1, heads),
-        norm_gain.reshape(1, width), kv_weight, cross_query,
+        query, key, value, gate_logit.T, exponent.reshape(1, heads),
+        norm_gain.reshape(heads, HD), kv_weight, cross_query,
     )
 
 

time: 66.7 us -> 63.4 us (0.951)
  local copies, waits for them, and re-layouts: 7.49 us -> 3.44 us
  Pallas kernels: 58.2 us -> 59.1 us
    unnamed x13 -> x2, local copies, waits for them, and re-layouts: 6.79 us -> 3.44 us
    pallas_call x1, Pallas kernels: 58.2 us -> 59.1 us  [body(): pl.pallas_call(functools.partial(kernel, nz, nhg), out_shape=(jax.ShapeDt...]
    reshape x1 -> x0, local copies, waits for them, and re-layouts: 0.7 us -> none  [body(): norm_gain.reshape(1, width)]
where the time goes in v2:
time: 63.4 us; the launch traced here: 63.2 us
  Pallas kernels  59.1 us (93%)
  local copies, waits for them, and re-layouts  3.44 us (5%)
  between operations  0.64 us (1%)
    pallas_call x1, Pallas kernels, body(): pl.pallas_call(functools.partial(kernel, nz, nhg), out_shape=(jax.ShapeDt...  59.1 us
    unnamed x2, local copies, waits for them, and re-layouts  3.44 us

profile of v2, /device:TPU:28, one launch (start us, length us, event | category | flops | bytes accessed | tf_op | source)
XLA Modules:
  0.0 63.2 jit_solution(10648119072670163701)
XLA Ops:
  0.6 59.1 %shard_map.95 = (bf16[128,1280]{1,0:T(8,128)(2,1)}, bf16[128,1280]{1,0:T(8,128)(2,1)}) custom-call(bf16[128,1280]{1,0:T(8,128)(2,1)} %q_hbm.1, bf16[128,1280]{1,0:T(8,128)(2,1)} %k_hbm.1, bf16[128,1280]{1,0:T(8,128)(2,1)} %v_hbm.1, f32[10,128]{1,0:T(8,128)} %bitcast.3, s32[1,10]{1,0:T(1,128)} %bitcast.5, f32[10,128]{1,0:T(8,128)} %bitcast.4, ...), custom_call_target="tpu_custom_call" | custom-call | tf_op jit(solution)/shard_map/pallas_call | solution.py:365
  59.7 1.7 %copy.12 = bf16[128,1280]{1,0:T(8,128)(2,1)} copy(bf16[128,1280]{1,0:T(8,128)(2,1)} %get-tuple-element.4) | data formatting | bytes 655360
  61.5 1.7 %copy.13 = bf16[128,1280]{1,0:T(8,128)(2,1)} copy(bf16[128,1280]{1,0:T(8,128)(2,1)} %get-tuple-element.5) | data formatting | bytes 655360

commit v3 on v2

--- a/solution.py
+++ b/solution.py
@@ -17,6 +17,11 @@
     return lax.dot_general(a, b, (dims, ((), ())), preferred_element_type=F32)
 
 
+def carry(q, state):
+    hi, lo = split(state)
+    return dot(q, hi) + dot(q, lo)
+
+
 def split(x):
     hi = x.astype(BF16)
     return hi, (x - hi.astype(F32)).astype(BF16)
@@ -25,13 +30,13 @@
 def kernel(
     nz, nhg,
     q_hbm, k_hbm, v_hbm, gate_hbm, expo_hbm, gain_hbm, w_hbm, cq_hbm,
-    ret_ref, att_ref,
-    q_ref, k_ref, v_ref, cq_ref, gate_ref, expo_ref, gain_ref, gate_pad,
+    ret_hbm, att_hbm,
+    ret_ref, att_ref, q_ref, k_ref, v_ref, cq_ref, gate_ref, expo_ref, gain_ref, gate_pad,
     w_vm, bcol, brow, dtot_ref, local_ref,
-    own_f, send_f, recv_f, send_s, recv_s, send_e, recv_e,
+    own_f, send_f, recv_f, recv_d, send_s, recv_s, send_e, recv_e,
     p1_send, p1_recv, p2_send, p2_recv, own_p,
     kv, cross, top_ref, den_ref, acc_ref,
-    in_sem, fs, fr, ss, sr, es, er, p1s, p1r, p2s, p2r, zs, zr, ys, yr,
+    in_sem, out_sem, d_sem, fs, fr, ss, sr, es, er, p1s, p1r, p2s, p2r, zs, zr, ys, yr,
 ):
     tok, width = q_ref.shape
     heads = width // HD
@@ -106,30 +111,34 @@
     brow[...] = jnp.transpose(cumul)
     for h in range(heads):
         bcol[h] = jnp.broadcast_to(cumul[:, h : h + 1], (tok, HD))
-        dtot_ref[h] = jnp.broadcast_to(jnp.exp(cumul[tok - 1 : tok, h : h + 1]), (8, HD))
-
-    def fresh(h, out, j):
+
+    pad = dtot_ref.shape[0]
+    dtot_ref[...] = jnp.exp(jnp.broadcast_to(brow[:pad, tok - 1 : tok], (pad, HD)))
+
+    def fresh(h):
         total = bcol[h, tok - 1 : tok, :]
         keys = k_ref[:, cols(h)].astype(F32) * (jnp.exp(total - bcol[h]) * scale)
         hi, lo = split(keys)
         vals = v_ref[:, cols(h)]
         dims = ((0,), (0,))
-        out[j, :HD, :] = dot(hi, vals, dims) + dot(lo, vals, dims)
-        out[j, HD:, :] = dtot_ref[h]
+        return dot(hi, vals, dims) + dot(lo, vals, dims)
 
     pl.semaphore_wait(barrier, 3 + jnp.where(first, 0, 1) + jnp.where(last, 0, 1))
 
     k_copy.wait()
     v_copy.wait()
+    d_copy = send(dtot_ref, recv_d, d_sem.at[0], d_sem.at[1], partner)
+    d_copy.start()
     for j in range(half):
-        fresh((1 - y) * half + j, send_f, j)
+        send_f[j] = fresh((1 - y) * half + j)
         send(send_f.at[j], recv_f.at[j], fs.at[j], fr.at[j], partner).start()
     for j in range(half):
-        fresh(y * half + j, own_f, j)
+        own_f[j] = fresh(y * half + j)
 
     def pair(j):
-        mine, his = own_f[j, :HD, :], recv_f[j, :HD, :]
-        dm, dh = own_f[j, HD : HD + 1, :], recv_f[j, HD : HD + 1, :]
+        mine, his = own_f[j], recv_f[j]
+        row = pl.ds(y * half + j, 1)
+        dm, dh = dtot_ref[row, :], recv_d[row, :]
         even = y == 0
         f0, f1 = jnp.where(even, mine, his), jnp.where(even, his, mine)
         d0, d1 = jnp.where(even, dm, dh), jnp.where(even, dh, dm)
@@ -148,6 +157,7 @@
     def _():
         recv_s[...] = jnp.zeros_like(recv_s)
 
+    d_copy.wait()
     for j in range(half):
         f_copy(j).wait_recv()
         f0, f1, d0, d1 = pair(j)
@@ -176,9 +186,7 @@
     acc_ref[...] = jnp.zeros_like(acc_ref)
 
     def finish(h, state):
-        hi, lo = split(state)
-        qh = q_ref[:, cols(h)]
-        out = local_ref[h] + (dot(qh, hi) + dot(qh, lo)) * jnp.exp(bcol[h])
+        out = local_ref[h] + carry(q_ref[:, cols(h)], state) * jnp.exp(bcol[h])
         mean = jnp.mean(out, axis=-1, keepdims=True)
         out = out - mean
         var = jnp.mean(out * out, axis=-1, keepdims=True)
@@ -211,6 +219,8 @@
     for j in range(half - lag, half):
         finish((1 - y) * half + j, recv_e[j])
 
+    ret_copy = pltpu.make_async_copy(ret_ref, ret_hbm, out_sem.at[kvh])
+    ret_copy.start()
     w_copy.wait()
     wide = 2 * HD
 
@@ -224,17 +234,19 @@
         return dot(ret_ref[...], w_vm[:, cols(dest * kvh + c, wide)])
 
     for c in range(kvh):
-        for b, dest in ((0, g3), (1, g1)):
-            p1_send[c, b] = part(dest, c)
-            p1_copy(c, b).start()
+        p1_send[c, 0] = part(g3, c)
+        p1_copy(c, 0).start()
     for c in range(kvh):
         p2_send[c] = part(g2, c)
-    for c in range(kvh):
         p1_copy(c, 0).wait_recv()
         p2_send[c] = p2_send[c] + p1_recv[c, 0]
         p2_copy(c).start()
     for c in range(kvh):
+        p1_send[c, 1] = part(g1, c)
+        p1_copy(c, 1).start()
+    for c in range(kvh):
         own_p[c] = part(g, c)
+    for c in range(kvh):
         p1_copy(c, 1).wait_recv()
         own_p[c] = own_p[c] + p1_recv[c, 1]
 
@@ -272,7 +284,20 @@
         den_ref[c] = den_ref[c] * factor + (expo[:, :HD] + expo[:, HD:])
         acc_ref[c] = acc_ref[c] * factor + dot(expo.astype(BF16), vals)
 
-    def earlier(zz, carry):
+    for c in range(kvh):
+        p2_copy(c).wait_recv()
+        spot(me, c)[...] = (own_p[c] + p2_recv[c]).astype(BF16)
+
+        @pl.when(y == 0)
+        def _():
+            y_copy(z, c).start()
+            spot(me + 1, c)[...] = jnp.zeros((tok, wide), BF16)
+
+        @pl.when(jnp.logical_not(last))
+        def _():
+            z_copy(z, c).start()
+
+    def relay(zz):
         for c in range(kvh):
             z_copy(zz, c).wait_recv()
 
@@ -281,29 +306,15 @@
                 z_copy(zz, c).start()
 
             y_copy(zz, c).start()
+
+    def use(zz):
         for c in range(kvh):
             y_arrived(zz, c).wait_recv()
             attend(zz, c, False)
-        return carry
-
-    lax.fori_loop(0, z - 1, earlier, 0)
-
-    for c in range(kvh):
-        p2_copy(c).wait_recv()
-        spot(me, c)[...] = (own_p[c] + p2_recv[c]).astype(BF16)
-
-        @pl.when(y == 0)
-        def _():
-            y_copy(z, c).start()
-            spot(me + 1, c)[...] = jnp.zeros((tok, wide), BF16)
-
-        @pl.when(jnp.logical_not(last))
-        def _():
-            z_copy(z, c).start()
 
     @pl.when(jnp.logical_not(first))
     def _():
-        earlier(z - 1, 0)
+        relay(z - 1)
 
     for c in range(kvh):
         @pl.when(y == 1)
@@ -311,12 +322,33 @@
             y_arrived(z, c).wait_recv()
 
         attend(z, c, True)
+
+    def step(n, carry):
+        relay(z - n)
+        use(z - n + 1)
+        return carry
+
+    lax.fori_loop(2, z + 1, step, 0)
+
+    @pl.when(jnp.logical_not(first))
+    def _():
+        use(0)
+
+    def att_copy(c):
+        at = slice(c * group * HD, (c + 1) * group * HD)
+        return pltpu.make_async_copy(att_ref.at[:, at], att_hbm.at[:, at], out_sem.at[c])
+
     for h in range(heads):
         c, i = h // group, h % group
         at = slice(i * tok, (i + 1) * tok)
         total = jnp.sum(den_ref[c, at, :], axis=-1, keepdims=True)
         att_ref[:, h * HD : (h + 1) * HD] = (acc_ref[c, at, :] / total).astype(BF16)
-
+        if i == group - 1:
+            att_copy(c).start()
+
+    ret_copy.wait()
+    for c in range(kvh):
+        att_copy(c).wait()
     for j in range(half):
         f_copy(j).wait_send()
         e_copy(j).wait_send()
@@ -349,6 +381,19 @@
         return carry
 
     lax.fori_loop(0, z, drain, 0)
+
+
+def hand_over(ret_in, att_in, ret_out, att_out, sem):
+    copies = []
+    rows = ret_in.shape[0] // 2
+    for i, (src, dst) in enumerate(((ret_in, ret_out), (att_in, att_out))):
+        for j in range(2):
+            at = pl.ds(j * rows, rows)
+            copies.append(pltpu.make_async_copy(src.at[at], dst.at[at], sem.at[i, j]))
+    for copy in copies:
+        copy.start()
+    for copy in copies:
+        copy.wait()
 
 
 def body(nctx, nhg, query, key, value, gate_logit, exponent, norm_gain, kv_weight, cross_query):
@@ -359,18 +404,19 @@
     share = kv_weight.shape[1] // nhg
     kvh = share // (2 * HD)
     rows = heads // kvh * tok
-    vmem = pl.BlockSpec(memory_space=pltpu.VMEM)
     hbm = pl.BlockSpec(memory_space=pltpu.HBM)
     dma = pltpu.SemaphoreType.DMA
-    return pl.pallas_call(
+    results = pl.pallas_call(
         functools.partial(kernel, nz, nhg),
         out_shape=(
             jax.ShapeDtypeStruct((tok, width), BF16),
             jax.ShapeDtypeStruct((tok, width), BF16),
         ),
         in_specs=[hbm] * 8,
-        out_specs=(vmem, vmem),
+        out_specs=(hbm, hbm),
         scratch_shapes=[
+            pltpu.VMEM((tok, width), BF16),
+            pltpu.VMEM((tok, width), BF16),
             pltpu.VMEM((tok, width), BF16),
             pltpu.VMEM((tok, width), BF16),
             pltpu.VMEM((tok, width), BF16),
@@ -382,11 +428,12 @@
             pltpu.VMEM(kv_weight.shape, BF16),
             pltpu.VMEM((heads, tok, HD), F32),
             pltpu.VMEM((HD, tok), F32),
-            pltpu.VMEM((heads, 8, HD), F32),
+            pltpu.VMEM((-(-heads // 8) * 8, HD), F32),
             pltpu.VMEM((heads, tok, HD), F32),
-            pltpu.VMEM((half, HD + 8, HD), F32),
-            pltpu.VMEM((half, HD + 8, HD), F32),
-            pltpu.VMEM((half, HD + 8, HD), F32),
+            pltpu.VMEM((half, HD, HD), F32),
+            pltpu.VMEM((half, HD, HD), F32),
+            pltpu.VMEM((half, HD, HD), F32),
+            pltpu.VMEM((-(-heads // 8) * 8, HD), F32),
             pltpu.VMEM((half, HD, HD), F32),
             pltpu.VMEM((half, HD, HD), F32),
             pltpu.VMEM((half, HD, HD), F32),
@@ -402,6 +449,8 @@
             pltpu.VMEM((kvh, rows, HD), F32),
             pltpu.VMEM((kvh, rows, HD), F32),
             dma((8,)),
+            dma((1 + kvh,)),
+            dma((2,)),
             dma((half,)), dma((half,)), dma((half,)), dma((half,)), dma((half,)), dma((half,)),
             dma((kvh, 2)), dma((kvh, 2)), dma((kvh,)), dma((kvh,)),
             dma((nz, kvh)), dma((nz, kvh)), dma((nz, kvh)), dma((nz, kvh)),
@@ -413,6 +462,17 @@
         query, key, value, gate_logit.T, exponent.reshape(1, heads),
         norm_gain.reshape(heads, HD), kv_weight, cross_query,
     )
+    return pl.pallas_call(
+        hand_over,
+        out_shape=(
+            jax.ShapeDtypeStruct((tok, width), BF16),
+            jax.ShapeDtypeStruct((tok, width), BF16),
+        ),
+        in_specs=[hbm, hbm],
+        out_specs=(hbm, hbm),
+        scratch_shapes=[dma((2, 2))],
+        compiler_params=pltpu.CompilerParams(vmem_limit_bytes=56 * 1024 * 1024),
+    )(*results)
 
 
 def solution(mesh):

time: 63.4 us -> 73.6 us (1.16)
  Pallas kernels: 59.1 us -> 72.8 us
  local copies, waits for them, and re-layouts: 3.44 us -> 0 us
    pallas_call x0 -> x1, Pallas kernels: none -> 21 us  [body(): pl.pallas_call(hand_over, out_shape=(jax.ShapeDtypeStruct((tok, width), B...]
    pallas_call x1, Pallas kernels: 59.1 us -> 51.8 us  [body(): pl.pallas_call(functools.partial(kernel, nz, nhg), out_shape=(jax.ShapeDt...]
    unnamed x2 -> x0, local copies, waits for them, and re-layouts: 3.44 us -> none
where the time goes in v3:
time: 73.6 us; the launch traced here: 73.4 us
  Pallas kernels  72.8 us (99%)
    pallas_call x1, Pallas kernels, body(): pl.pallas_call(functools.partial(kernel, nz, nhg), out_shape=(jax.ShapeDt...  51.8 us
    pallas_call x1, Pallas kernels, body(): pl.pallas_call(hand_over, out_shape=(jax.ShapeDtypeStruct((tok, width), B...  21 us

profile of v3, /device:TPU:28, one launch (start us, length us, event | category | flops | bytes accessed | tf_op | source)
XLA Modules:
  0.0 73.4 jit_solution(6386183698523839796)
XLA Ops:
  0.6 51.8 %shard_map.95 = (bf16[128,1280]{1,0:T(8,128)(2,1)}, bf16[128,1280]{1,0:T(8,128)(2,1)}) custom-call(bf16[128,1280]{1,0:T(8,128)(2,1)} %q_hbm.1, bf16[128,1280]{1,0:T(8,128)(2,1)} %k_hbm.1, bf16[128,1280]{1,0:T(8,128)(2,1)} %v_hbm.1, f32[10,128]{1,0:T(8,128)} %bitcast.3, s32[1,10]{1,0:T(1,128)} %bitcast.5, f32[10,128]{1,0:T(8,128)} %bitcast.4, ...), custom_call_target="tpu_custom_call" | custom-call | tf_op jit(solution)/shard_map/pallas_call | solution.py:409
  52.4 21.0 %shard_map.96 = (bf16[128,1280]{1,0:T(8,128)(2,1)}, bf16[128,1280]{1,0:T(8,128)(2,1)}) custom-call(bf16[128,1280]{1,0:T(8,128)(2,1)} %get-tuple-element.4.ret_in, bf16[128,1280]{1,0:T(8,128)(2,1)} %get-tuple-element.5.att_in), custom_call_target="tpu_custom_call" | custom-call | tf_op jit(solution)/shard_map/pallas_call | solution.py:465

commit v4 on v3

--- a/solution.py
+++ b/solution.py
@@ -383,17 +383,24 @@
     lax.fori_loop(0, z, drain, 0)
 
 
-def hand_over(ret_in, att_in, ret_out, att_out, sem):
-    copies = []
+def hand_over(ret_in, att_in, ret_out, att_out, held, in_sem, out_sem):
+    moves = []
     rows = ret_in.shape[0] // 2
     for i, (src, dst) in enumerate(((ret_in, ret_out), (att_in, att_out))):
         for j in range(2):
             at = pl.ds(j * rows, rows)
-            copies.append(pltpu.make_async_copy(src.at[at], dst.at[at], sem.at[i, j]))
-    for copy in copies:
-        copy.start()
-    for copy in copies:
-        copy.wait()
+            spot = held.at[i, at]
+            moves.append((
+                pltpu.make_async_copy(src.at[at], spot, in_sem.at[i, j]),
+                pltpu.make_async_copy(spot, dst.at[at], out_sem.at[i, j]),
+            ))
+    for load, _ in moves:
+        load.start()
+    for load, store in moves:
+        load.wait()
+        store.start()
+    for _, store in moves:
+        store.wait()
 
 
 def body(nctx, nhg, query, key, value, gate_logit, exponent, norm_gain, kv_weight, cross_query):
@@ -470,7 +477,7 @@
         ),
         in_specs=[hbm, hbm],
         out_specs=(hbm, hbm),
-        scratch_shapes=[dma((2, 2))],
+        scratch_shapes=[pltpu.VMEM((2, tok, width), BF16), dma((2, 2)), dma((2, 2))],
         compiler_params=pltpu.CompilerParams(vmem_limit_bytes=56 * 1024 * 1024),
     )(*results)
 

time: 73.6 us -> 54.5 us (0.74)
  Pallas kernels: 72.8 us -> 53.7 us
    pallas_call x1, Pallas kernels: 21 us -> 1.89 us  [body(): pl.pallas_call(hand_over, out_shape=(jax.ShapeDtypeStruct((tok, width), B...]
where the time goes in v4:
time: 54.5 us; the launch traced here: 54.3 us
  Pallas kernels  53.7 us (99%)
  between operations  0.64 us (1%)
    pallas_call x1, Pallas kernels, body(): pl.pallas_call(functools.partial(kernel, nz, nhg), out_shape=(jax.ShapeDt...  51.8 us
    pallas_call x1, Pallas kernels, body(): pl.pallas_call(hand_over, out_shape=(jax.ShapeDtypeStruct((tok, width), B...  1.89 us

profile of v4, /device:TPU:28, one launch (start us, length us, event | category | flops | bytes accessed | tf_op | source)
XLA Modules:
  0.0 54.3 jit_solution(6013083653077304302)
XLA Ops:
  0.6 51.8 %shard_map.95 = (bf16[128,1280]{1,0:T(8,128)(2,1)}, bf16[128,1280]{1,0:T(8,128)(2,1)}) custom-call(bf16[128,1280]{1,0:T(8,128)(2,1)} %q_hbm.1, bf16[128,1280]{1,0:T(8,128)(2,1)} %k_hbm.1, bf16[128,1280]{1,0:T(8,128)(2,1)} %v_hbm.1, f32[10,128]{1,0:T(8,128)} %bitcast.3, s32[1,10]{1,0:T(1,128)} %bitcast.5, f32[10,128]{1,0:T(8,128)} %bitcast.4, ...), custom_call_target="tpu_custom_call" | custom-call | tf_op jit(solution)/shard_map/pallas_call | solution.py:416
  52.4 1.9 %shard_map.96 = (bf16[128,1280]{1,0:T(8,128)(2,1)}, bf16[128,1280]{1,0:T(8,128)(2,1)}) custom-call(bf16[128,1280]{1,0:T(8,128)(2,1)} %get-tuple-element.4.ret_in, bf16[128,1280]{1,0:T(8,128)(2,1)} %get-tuple-element.5.att_in), custom_call_target="tpu_custom_call" | custom-call | tf_op jit(solution)/shard_map/pallas_call | solution.py:472
